TPU v7x, 32 devices: a whole 2x2x4 slice. The times are simulated.
32 devices in a mesh: ctx: 8 (over y, x, core), fsdp: 4 (over z).
Axes of the slice: x: 2, y: 2, z: 4, core: 2. Of those that a mesh axis runs over, the one named last changes fastest.
Arguments:
- tokens_in: bfloat16 [4096, 5376], P('ctx'), may hold values from -6 to 6
- query: bfloat16 [4096, 1024], P('ctx', 'fsdp'), may hold values from -6 to 6
- key: bfloat16 [4096, 512], P('ctx', 'fsdp'), may hold values from -6 to 6
- value: bfloat16 [4096, 512], P('ctx', 'fsdp'), may hold values from -6 to 6
- d_out: bfloat16 [4096, 1024], P('ctx', 'fsdp'), may hold values from -6 to 6
- seg_ids: int32 [4096], P('ctx'), may hold values from 0 to 3, as said below
Outputs:
- d_query: bfloat16 [4096, 1024], P('ctx', 'fsdp')
- d_key: bfloat16 [4096, 512], P('ctx', 'fsdp')
- d_value: bfloat16 [4096, 512], P('ctx', 'fsdp')
- dw_key: float32 [5376, 512], P('ctx', 'fsdp')
- dw_value: float32 [5376, 512], P('ctx', 'fsdp')
Inputs may be any that keep to these rules, and one draw needn't show every extreme that they name: `seg_ids`: never falls along the sequence, starts at 0 and rises by at most one from a token to the next; every segment number is used.
All inputs are finite; a program needn't handle non-finite values.
Results may differ from a plain program's by a relative error of at most 0.014.
Values may be sent and summed in bfloat16 or wider, within the bound.
A program may use at most 64 MiB of HBM per device.

v0:
```python
from functools import partial

import jax
import jax.numpy as jnp
from jax import lax
from jax.sharding import PartitionSpec as P

HD = 128
GROUP = 2
WINDOW = 1024


query_scale = 168.0 ** (-0.5)
masked_score = -1e30


def shifted(array, axis, by):
    length = lax.axis_size(axis)
    pairs = [(i, i + by) for i in range(length) if 0 <= i + by < length]
    return lax.ppermute(array, axis, pairs)


def block_scores(q_heads, keys, allowed):
    scores = (
        jnp.einsum("ihgd,jhd->hgij", q_heads, keys, preferred_element_type=jnp.float32)
        * query_scale
    )
    return jnp.where(allowed[None, None], scores, masked_score)


def block_grads(q_heads, grad_heads, delta_col, probs, probs_b, keys, values):
    rows = keys.shape[0]
    width = keys.shape[1] * keys.shape[2]
    dprob = jnp.einsum("ihgd,jhd->hgij", grad_heads, values, preferred_element_type=jnp.float32)
    dscore = (probs * (dprob - delta_col)).astype(jnp.bfloat16)
    dq_part = jnp.einsum("hgij,jhd->ihgd", dscore, keys, preferred_element_type=jnp.float32)
    dk_part = (
        jnp.einsum("hgij,ihgd->jhd", dscore, q_heads, preferred_element_type=jnp.float32)
        * query_scale
    )
    dv_part = jnp.einsum("hgij,ihgd->jhd", probs_b, grad_heads, preferred_element_type=jnp.float32)
    contrib = jnp.concatenate([dk_part.reshape(rows, width), dv_part.reshape(rows, width)], 1)
    return (dq_part, contrib)


def body(tokens_in, query, key, value, d_out, seg_ids):
    rows = query.shape[0]
    kv_width = key.shape[1]
    heads = kv_width // HD
    hops = WINDOW // rows
    here = lax.axis_index("ctx")
    q_heads = query.reshape(rows, heads, GROUP, HD)
    grad_heads = d_out.reshape(rows, heads, GROUP, HD)
    paired = jnp.concatenate([key, value], 1)
    blocks = [(paired, seg_ids)]
    for hop in range(1, hops + 1):
        blocks.append(shifted((paired, seg_ids), "ctx", hop))
    offsets = jnp.arange(rows, dtype=jnp.int32)
    q_pos = here * rows + offsets
    masks = []
    key_list = []
    value_list = []
    for hop in range(hops + 1):
        block_pair, block_seg = blocks[hop]
        k_pos = (here - hop) * rows + offsets
        allowed = (k_pos[None, :] <= q_pos[:, None]) & (q_pos[:, None] - k_pos[None, :] < WINDOW)
        allowed = allowed & (k_pos[None, :] >= 0) & (seg_ids[:, None] == block_seg[None, :])
        masks.append(allowed)
        key_list.append(block_pair[:, :kv_width].reshape(rows, heads, HD))
        value_list.append(block_pair[:, kv_width:].reshape(rows, heads, HD))
    score_list = []
    for hop in range(hops + 1):
        score_list.append(block_scores(q_heads, key_list[hop], masks[hop]))
    top = score_list[0].max(-1, keepdims=True)
    for hop in range(1, hops + 1):
        top = jnp.maximum(top, score_list[hop].max(-1, keepdims=True))
    expo_list = [jnp.exp(scores - top) for scores in score_list]
    total = expo_list[0].sum(-1, keepdims=True)
    for hop in range(1, hops + 1):
        total = total + expo_list[hop].sum(-1, keepdims=True)
    probs_list = [expo / total for expo in expo_list]
    probs_b_list = [probs.astype(jnp.bfloat16) for probs in probs_list]
    attended = jnp.zeros((rows, heads, GROUP, HD), jnp.float32)
    for hop in range(hops + 1):
        attended = attended + jnp.einsum(
            "hgij,jhd->ihgd", probs_b_list[hop], value_list[hop], preferred_element_type=jnp.float32
        )
    delta = jnp.sum(grad_heads.astype(jnp.float32) * attended, -1)
    delta_col = jnp.transpose(delta, (1, 2, 0))[..., None]
    dq_total = jnp.zeros((rows, heads, GROUP, HD), jnp.float32)
    contribs = []
    for hop in range(hops + 1):
        compute = partial(
            block_grads,
            q_heads,
            grad_heads,
            delta_col,
            probs_list[hop],
            probs_b_list[hop],
            key_list[hop],
            value_list[hop],
        )
        dq_part, contrib = compute()
        dq_total = dq_total + dq_part
        contribs.append(contrib)
    grads_total = contribs[0]
    for hop in range(1, hops + 1):
        grads_total = grads_total + shifted(contribs[hop].astype(jnp.bfloat16), "ctx", -hop).astype(
            jnp.float32
        )
    grads_both = grads_total.astype(jnp.bfloat16)
    d_query = (dq_total * query_scale).astype(jnp.bfloat16).reshape(rows, heads * GROUP * HD)
    d_key = grads_both[:, :kv_width]
    d_value = grads_both[:, kv_width:]
    summed = lax.psum_scatter(
        lax.dot_general(
            tokens_in, grads_both, (((0,), (0,)), ((), ())), preferred_element_type=jnp.float32
        ).astype(jnp.bfloat16),
        "ctx",
        scatter_dimension=0,
        tiled=True,
    ).astype(jnp.float32)
    dw_key = summed[:, :kv_width]
    dw_value = summed[:, kv_width:]
    return (d_query, d_key, d_value, dw_key, dw_value)


def solution(mesh):
    in_specs = (
        P("ctx", None),
        P("ctx", "fsdp"),
        P("ctx", "fsdp"),
        P("ctx", "fsdp"),
        P("ctx", "fsdp"),
        P("ctx"),
    )
    out_specs = (
        P("ctx", "fsdp"),
        P("ctx", "fsdp"),
        P("ctx", "fsdp"),
        P("ctx", "fsdp"),
        P("ctx", "fsdp"),
    )
    return jax.shard_map(body, mesh=mesh, in_specs=in_specs, out_specs=out_specs, check_vma=False)
```

profile of v0, /device:TPU:0, one launch (start us, length us, event | category | flops | bytes accessed | tf_op | source)
XLA Modules:
  0.0 116.8 jit_solution(9800281069353978694)
XLA Ops:
  7.2 0.0 reduce-scatter.4.cloned.1.call-start
  7.2 2.5 %collective-permute-start = (s32[512]{0:T(512)}, s32[512]{0:T(512)S(1)}, u32[]{:S(2)}, u32[]{:S(2)}) collective-permute-start(s32[512]{0:T(512)} %param.11), channel_id=1, source_target_pairs={{0,4},{4,8},{8,12},{12,16},{16,20},{20,24},{24,28},{1,5},{5,9},{9,... | collective-permute-start | bytes 6152 | tf_op jit(solution)/shard_map/ppermute | solution.py:20
  9.7 4.4 %collective-permute-start.2 = (s32[512]{0:T(512)}, s32[512]{0:T(512)S(1)}, u32[]{:S(2)}, u32[]{:S(2)}) collective-permute-start(s32[512]{0:T(512)} %param.11), channel_id=1, source_target_pairs={{0,8},{4,12},{8,16},{12,20},{16,24},{20,28},{1,9},{5,13},{9,17},{1... | collective-permute-start | bytes 6152 | tf_op jit(solution)/shard_map/ppermute | solution.py:20
  14.1 0.9 constant_dynamic-update-slice_fusion.1
  15.1 0.9 constant_dynamic-update-slice_fusion
  16.0 3.4 %collective-permute-start.3 = (bf16[512,256]{1,0:T(8,128)(2,1)S(1)}, bf16[512,256]{1,0:T(8,128)(2,1)S(1)}, u32[]{:S(2)}, u32[]{:S(2)}) collective-permute-start(bf16[512,256]{1,0:T(8,128)(2,1)S(1)} %constant_dynamic-update-slice_fusion), channel_id=1, source_target_pairs={{0,8},{4,12},{8,16},{12,20},{16,24},{20,28},{1,9},{5,13},{9,17},{1... | collective-permute-start | bytes 786440 | tf_op jit(solution)/shard_map/ppermute | solution.py:20
  19.4 3.0 %collective-permute-start.1 = (bf16[512,256]{1,0:T(8,128)(2,1)S(1)}, bf16[512,256]{1,0:T(8,128)(2,1)S(1)}, u32[]{:S(2)}, u32[]{:S(2)}) collective-permute-start(bf16[512,256]{1,0:T(8,128)(2,1)S(1)} %constant_dynamic-update-slice_fusion), channel_id=1, source_target_pairs={{0,4},{4,8},{8,12},{12,16},{16,20},{20,24},{24,28},{1,5},{5,9},{9,... | collective-permute-start | bytes 786440 | tf_op jit(solution)/shard_map/ppermute | solution.py:20
  22.5 1.1 copy.110
  23.6 0.0 copy-start.1
  23.6 1.2 %copy.51 = f32[512,256]{0,1:T(8,128)S(1)} copy(bf16[512,256]{1,0:T(8,128)(2,1)} %param.10) | data formatting | bytes 786432 | tf_op jit(solution)/shard_map/convert_element_type | solution.py:88
  24.8 1.1 copy.109
  25.9 0.0 collective-permute-done
  25.9 0.0 collective-permute-done.2
  25.9 0.0 copy-done.7
  25.9 1.5 %fusion.44 = (pred[512,512]{0,1:T(8,128)(4,1)S(1)}, pred[512,512]{0,1:T(8,128)(4,1)S(1)}, pred[512,512]{0,1:T(8,128)(4,1)S(1)}) fusion(s32[512]{0:T(512)S(1)} %copy-done.7, s32[512]{0:T(512)S(1)} %iota_add_fusion.2, s32[512]{0:T(512)S(1)} %collective-permute-done, s32[512]{0:T(512)S(1)} %get-tuple-element.32, pred[512]{0:T(512)(128)(4,1)S(1)} %get-tuple-element.34, ...), kind=kLoop, calls=%fused_computation.67 | loop fusion | flops 5505024 | bytes 800256 | tf_op jit(solution)/shard_map/and | solution.py:67
  27.4 0.0 copy-done
  27.4 0.5 fusion.66
  28.0 0.0 collective-permute-done.3
  28.0 0.0 copy-start.5
  28.0 0.5 fusion.14
  28.5 0.0 collective-permute-done.1
  28.6 0.0 copy-start.3
  28.6 0.5 fusion.13
  29.1 1.3 %fusion.10 = (f32[2,512]{1,0:T(2,128)S(1)}, f32[2,512]{1,0:T(2,128)S(1)}, f32[2,512]{1,0:T(2,128)S(1)}) fusion(f32[512,512,2]{1,0,2:T(8,128)S(1)} %get-tuple-element.30, f32[2,512]{1,0:T(2,128)S(1)} %maximum_maximum_fusion, pred[512,512]{0,1:T(8,128)(4,1)S(1)} %get-tuple-element.22, f32[512,512,2]{1,0,2:T(8,128)S(1)} %get-tuple-element.26, ...), kind=kLoop, calls=%fused_computation.20 | loop fusion | flops 5239808 | bytes 6832128 | tf_op jit(solution)/shard_map/reduce_sum | solution.py:80
  30.4 0.3 fusion.50
  30.7 0.8 fusion.28
  31.5 0.0 copy-start.2
  31.5 0.8 fusion.29
  32.3 0.1 copy-done.2
  32.4 0.3 convolution_bitcast_fusion.1
  32.8 0.5 convolution_bitcast_fusion.6
  33.3 0.8 fusion.33
  34.1 0.8 fusion.24
  34.9 0.5 fusion.15
  35.4 0.0 copy-done.1
  35.4 0.0 copy-done.3
  35.4 0.0 copy-start.6
  35.5 0.8 fusion.16
  36.3 0.5 fusion.30
  36.8 0.0 slice-start
  36.8 0.0 slice-start.1
  36.8 1.6 %collective-permute-start.4 = (bf16[512,256]{0,1:T(8,128)(2,1)S(1)}, bf16[512,256]{0,1:T(8,128)(2,1)S(1)}, u32[]{:S(2)}, u32[]{:S(2)}) collective-permute-start(bf16[512,256]{0,1:T(8,128)(2,1)S(1)} %pad_maximum_fusion), channel_id=1, source_target_pairs={{4,0},{8,4},{12,8},{16,12},{20,16},{24,20},{28,24},{5,1},{9,5},{13... | collective-permute-start | bytes 786440 | tf_op jit(solution)/shard_map/ppermute | solution.py:20
  38.4 1.8 %fusion.17 = bf16[2,512,512]{1,2,0:T(8,128)(2,1)S(1)} fusion(bf16[512,2,128]{0,2,1:T(8,128)(2,1)} %bitcast.219, f32[2,512]{1,0:T(2,128)S(1)} %bitcast.225, f32[2,512]{1,0:T(2,128)S(1)} %add_add_fusion, f32[2,512]{1,0:T(2,128)S(1)} %maximum_maximum_fusion, f32[512,512,2]{1,0,2:T(8,128)S(1)} %get-tuple-element.26, ...), kind=kOutput, calls=%fused_computation.27 | convolution fusion | flops 137887744 | bytes 3813376 | tf_op jit(solution)/shard_map/ihgd,jhd->hgij/dot_general | solution.py:34
  40.2 0.5 fusion.31
  40.7 1.5 %collective-permute-start.5 = (bf16[512,256]{0,1:T(8,128)(2,1)S(1)}, bf16[512,256]{0,1:T(8,128)(2,1)S(1)}, u32[]{:S(2)}, u32[]{:S(2)}) collective-permute-start(bf16[512,256]{0,1:T(8,128)(2,1)S(1)} %pad_maximum_fusion.1), channel_id=1, source_target_pairs={{8,0},{12,4},{16,8},{20,12},{24,16},{28,20},{9,1},{13,5},{17,9},{2... | collective-permute-start | bytes 786440 | tf_op jit(solution)/shard_map/ppermute | solution.py:20
  42.2 0.5 fusion.27
  42.7 0.0 collective-permute-done.4
  42.7 10.3 %collective-permute-done.5 = bf16[512,256]{0,1:T(8,128)(2,1)S(1)} collective-permute-done((bf16[512,256]{0,1:T(8,128)(2,1)S(1)}, bf16[512,256]{0,1:T(8,128)(2,1)S(1)}, u32[]{:S(2)}, u32[]{:S(2)}) %collective-permute-start.5) | collective-permute-done | bytes 262176 | tf_op jit(solution)/shard_map/ppermute | solution.py:20
  53.0 0.1 fusion.52
  53.2 3.2 %fusion = bf16[5376,256]{0,1:T(8,128)(2,1)} fusion(bf16[512,256]{0,1:T(8,128)(2,1)S(1)} %fusion.52, bf16[512,5376]{1,0:T(8,128)(2,1)S(1)} %bitcast.222), kind=kOutput, calls=%fused_computation.1 | convolution fusion | flops 1410662400 | bytes 8519680 | tf_op jit(solution)/shard_map/dot_general | solution.py:116
  56.4 4.6 %copy.107 = bf16[5376,256]{1,0:T(8,128)(2,1)} copy(bf16[5376,256]{0,1:T(8,128)(2,1)} %fusion) | data formatting | bytes 5505024
  61.0 0.0 reduce-scatter.4.cloned.1.call-update
  61.0 0.0 copy-start.4
  61.0 0.3 convolution_bitcast_fusion
  61.4 1.2 %fusion.58 = f32[128,2,512]{2,0,1:T(8,128)S(1)} fusion(bf16[2,512,512]{1,2,0:T(8,128)(2,1)S(1)} %fusion.17, bf16[512,256]{1,0:T(8,128)(2,1)} %copy-done.5), kind=kOutput, calls=%fused_computation.88 | convolution fusion | flops 134217728 | bytes 1703936 | tf_op jit(solution)/shard_map/hgij,jhd->ihgd/dot_general | solution.py:36
  62.6 0.3 fusion.23
  63.0 0.8 copy.78
  63.8 0.8 copy.79
  64.6 0.8 copy.80
  65.4 41.6 %reduce-scatter.4.cloned.1.call-done = bf16[672,256]{1,0:T(8,128)(2,1)} async-done(((bf16[5376,256]{1,0:T(8,128)(2,1)}), bf16[672,256]{1,0:T(8,128)(2,1)}) %reduce-scatter.4.cloned.1.call-update) | async-done | bytes 344080
  106.9 1.1 copy.108
  108.1 0.1 fusion.64
  108.2 0.9 copy.81
  109.0 0.9 copy.82
  (17 shorter events, 0.1 us)
Async XLA Ops:
  7.2 18.7 %copy-start.7 = (s32[512]{0:T(512)S(1)}, s32[512]{0:T(512)}, u32[]{:S(2)}) copy-start(s32[512]{0:T(512)} %param.11) | copy-start | bytes 6148
  7.2 20.3 %copy-start = (bf16[512,128]{1,0:T(8,128)(2,1)S(1)}, bf16[512,128]{1,0:T(8,128)(2,1)}, u32[]{:S(2)}) copy-start(bf16[512,128]{1,0:T(8,128)(2,1)} %param.8) | copy-start | bytes 393220
  7.2 99.7 %reduce-scatter.4.cloned.1.call-start = ((), (), s32[]{:S(2)}) async-start(), calls=%async_computation.1 | async-start | bytes 3096576
  7.2 18.6 %collective-permute-start = (s32[512]{0:T(512)}, s32[512]{0:T(512)S(1)}, u32[]{:S(2)}, u32[]{:S(2)}) collective-permute-start(s32[512]{0:T(512)} %param.11), channel_id=1, source_target_pairs={{0,4},{4,8},{8,12},{12,16},{16,20},{20,24},{24,28},{1,5},{5,9},{9,... | collective-permute-start | bytes 6152 | tf_op jit(solution)/shard_map/ppermute | solution.py:20
  9.7 16.1 %collective-permute-start.2 = (s32[512]{0:T(512)}, s32[512]{0:T(512)S(1)}, u32[]{:S(2)}, u32[]{:S(2)}) collective-permute-start(s32[512]{0:T(512)} %param.11), channel_id=1, source_target_pairs={{0,8},{4,12},{8,16},{12,20},{16,24},{20,28},{1,9},{5,13},{9,17},{1... | collective-permute-start | bytes 6152 | tf_op jit(solution)/shard_map/ppermute | solution.py:20
  16.0 12.0 %collective-permute-start.3 = (bf16[512,256]{1,0:T(8,128)(2,1)S(1)}, bf16[512,256]{1,0:T(8,128)(2,1)S(1)}, u32[]{:S(2)}, u32[]{:S(2)}) collective-permute-start(bf16[512,256]{1,0:T(8,128)(2,1)S(1)} %constant_dynamic-update-slice_fusion), channel_id=1, source_target_pairs={{0,8},{4,12},{8,16},{12,20},{16,24},{20,28},{1,9},{5,13},{9,17},{1... | collective-permute-start | bytes 786440 | tf_op jit(solution)/shard_map/ppermute | solution.py:20
  19.4 9.1 %collective-permute-start.1 = (bf16[512,256]{1,0:T(8,128)(2,1)S(1)}, bf16[512,256]{1,0:T(8,128)(2,1)S(1)}, u32[]{:S(2)}, u32[]{:S(2)}) collective-permute-start(bf16[512,256]{1,0:T(8,128)(2,1)S(1)} %constant_dynamic-update-slice_fusion), channel_id=1, source_target_pairs={{0,4},{4,8},{8,12},{12,16},{16,20},{20,24},{24,28},{1,5},{5,9},{9,... | collective-permute-start | bytes 786440 | tf_op jit(solution)/shard_map/ppermute | solution.py:20
  23.6 11.9 %copy-start.1 = (bf16[512,256]{0,1:T(8,128)(2,1)}, bf16[512,256]{0,1:T(8,128)(2,1)S(1)}, u32[]{:S(2)}) copy-start(bf16[512,256]{0,1:T(8,128)(2,1)S(1)} %copy.110) | copy-start | bytes 786436
  28.0 5.3 %copy-start.5 = (bf16[512,256]{1,0:T(8,128)(2,1)}, bf16[512,256]{1,0:T(8,128)(2,1)S(1)}, u32[]{:S(2)}) copy-start(bf16[512,256]{1,0:T(8,128)(2,1)S(1)} %collective-permute-done.3) | copy-start | bytes 786436
  28.6 6.9 %copy-start.3 = (bf16[512,256]{1,0:T(8,128)(2,1)}, bf16[512,256]{1,0:T(8,128)(2,1)S(1)}, u32[]{:S(2)}) copy-start(bf16[512,256]{1,0:T(8,128)(2,1)S(1)} %collective-permute-done.1) | copy-start | bytes 786436
  31.5 0.9 copy-start.2
  35.4 3.0 %copy-start.6 = (bf16[512,256]{1,0:T(8,128)(2,1)S(1)}, bf16[512,256]{1,0:T(8,128)(2,1)}, u32[]{:S(2)}) copy-start(bf16[512,256]{1,0:T(8,128)(2,1)} %copy-done.5) | copy-start | bytes 786436
  36.8 16.4 %slice-start = ((s8[5505024]{0:T(1024)(128)(4,1)}), s8[4194304]{0:T(1024)(128)(4,1)S(1)}, s32[]{:S(2)}) async-start(s8[5505024]{0:T(1024)(128)(4,1)} %bitcast.221), calls=%async_computation.2 | async-start | bytes 8388608
  36.8 16.3 %slice-start.1 = ((s8[5505024]{0:T(1024)(128)(4,1)}), s8[1310720]{0:T(1024)(128)(4,1)S(1)}, s32[]{:S(2)}) async-start(s8[5505024]{0:T(1024)(128)(4,1)} %bitcast.221), calls=%async_computation.3 | async-start | bytes 2621440
  36.8 5.9 %collective-permute-start.4 = (bf16[512,256]{0,1:T(8,128)(2,1)S(1)}, bf16[512,256]{0,1:T(8,128)(2,1)S(1)}, u32[]{:S(2)}, u32[]{:S(2)}) collective-permute-start(bf16[512,256]{0,1:T(8,128)(2,1)S(1)} %pad_maximum_fusion), channel_id=1, source_target_pairs={{4,0},{8,4},{12,8},{16,12},{20,16},{24,20},{28,24},{5,1},{9,5},{13... | collective-permute-start | bytes 786440 | tf_op jit(solution)/shard_map/ppermute | solution.py:20
  40.7 12.3 %collective-permute-start.5 = (bf16[512,256]{0,1:T(8,128)(2,1)S(1)}, bf16[512,256]{0,1:T(8,128)(2,1)S(1)}, u32[]{:S(2)}, u32[]{:S(2)}) collective-permute-start(bf16[512,256]{0,1:T(8,128)(2,1)S(1)} %pad_maximum_fusion.1), channel_id=1, source_target_pairs={{8,0},{12,4},{16,8},{20,12},{24,16},{28,20},{9,1},{13,5},{17,9},{2... | collective-permute-start | bytes 786440 | tf_op jit(solution)/shard_map/ppermute | solution.py:20
  61.0 1.6 %copy-start.4 = (bf16[512,256]{1,0:T(8,128)(2,1)S(1)}, bf16[512,256]{1,0:T(8,128)(2,1)}, u32[]{:S(2)}) copy-start(bf16[512,256]{1,0:T(8,128)(2,1)} %copy-done.3) | copy-start | bytes 786436
Sparse Core Ops, SparseCore 0:
  61.1 45.7 reduce-scatter.3
where the time goes:
time: 117 us
  waiting for transfers between devices  51.9 us (44%)
  starting transfers between devices  16.3 us (14%)
  local copies, waits for them, and re-layouts  15.4 us (13%)
  matrix products  15.3 us (13%)
  between operations  14.5 us (12%)
  other arithmetic  3.3 us (3%)
    unnamed x2, waiting for transfers between devices  41.6 us
    ppermute x6, starting transfers between devices, shifted(): return lax.ppermute(array, axis, pairs)  16.3 us
    unnamed x28, local copies, waits for them, and re-layouts  11 us
    ppermute x6, waiting for transfers between devices, shifted(): return lax.ppermute(array, axis, pairs)  10.3 us
    dot_general x3, matrix products, block_grads(): jnp.einsum('ihgd,jhd->hgij', grad_heads, values, preferred_element_type=j...  3.19 us
    dot_general x1, matrix products, body(): lax.dot_general(tokens_in, grads_both, (((0,), (0,)), ((), ())), preferre...  3.19 us
  transfers between devices with their start and end apart: 7, of which 2 were waited for; matrix products, arithmetic and copies ran while one was open for 13% of the time, Pallas kernels for 0%

commit v1 on v0

v1 whole, which is shorter than its diff:
```python
import functools
import math

import jax
import jax.numpy as jnp
from jax import lax
from jax.experimental import pallas as pl
from jax.experimental.pallas import tpu as pltpu
from jax.sharding import PartitionSpec as P

HD = 128
WINDOW = 1024
TILE = 128

query_scale = 168.0 ** (-0.5)
masked_score = -1e30
EXP_SCALE = query_scale * math.log2(math.e)
F32 = jnp.float32
BF16 = jnp.bfloat16


def dot(a, b, contract):
    return lax.dot_general(a, b, ((contract[:1], contract[1:]), ((), ())), preferred_element_type=F32)


def kernel(n, fused, *refs):
    if fused:
        (seg_ref, q_ref, k_ref, v_ref, do_ref, x_hbm, dq_ref, dk_ref, dv_ref, dwk_ref, dwv_ref) = refs[:11]
        (kv, segs, segc, qs, dos, s_buf, dp_buf, pb, ds, dqt, out_g, in_g, kv_send, kv_recv, seg_send,
         seg_recv, g_send, g_recv, x_buf, xt, g_buf, one_out, one_in, two_out, two_in, three_out, three_in,
         one_send, one_recv, two_send, two_recv, three_send, three_recv, x_sem) = refs[11:]
    else:
        (seg_ref, q_ref, k_ref, v_ref, do_ref, dq_ref, dk_ref, dv_ref) = refs[:8]
        (kv, segs, segc, qs, dos, s_buf, dp_buf, pb, ds, dqt, out_g, in_g, kv_send, kv_recv, seg_send,
         seg_recv, g_send, g_recv) = refs[8:]
    me = lax.axis_index("ctx")
    rows = k_ref.shape[0]
    tiles = rows // TILE

    def remote(src, dst, send, recv, to):
        return pltpu.make_async_remote_copy(
            src_ref=src, dst_ref=dst, send_sem=send, recv_sem=recv,
            device_id={"ctx": to}, device_id_type=pl.DeviceIdType.MESH)

    if fused:
        x_copy = pltpu.make_async_copy(x_hbm, x_buf, x_sem)
        x_copy.start()
    barrier = pltpu.get_barrier_semaphore()
    near = [1, n - 1, 2, n - 2] + ([n // 2] if fused else [])
    for step in near:
        pl.semaphore_signal(barrier, inc=1, device_id={"ctx": lax.rem(me + step, n)},
                            device_id_type=pl.DeviceIdType.MESH)
    segs[0] = jnp.broadcast_to(seg_ref[...], (8, rows))
    kv[0, 0] = k_ref[...]
    kv[0, 1] = v_ref[...]
    pl.semaphore_wait(barrier, len(near))

    seg_copies, kv_copies = {}, {}
    for hop in (1, 2):
        to = lax.rem(me + hop, n)
        seg_copies[hop] = remote(segs.at[0], segs.at[hop], seg_send.at[hop - 1], seg_recv.at[hop - 1], to)
        for which in (0, 1):
            kv_copies[hop, which] = remote(kv.at[0, which], kv.at[hop, which], kv_send.at[hop - 1, which],
                                           kv_recv.at[hop - 1, which], to)
    for hop in (1, 2):
        seg_copies[hop].start()
    for which in (0, 1):
        for hop in (1, 2):
            kv_copies[hop, which].start()

    for head in (0, 1):
        qs[pl.ds(head * rows, rows), :] = q_ref[:, head * HD:(head + 1) * HD]
        dos[pl.ds(head * rows, rows), :] = do_ref[:, head * HD:(head + 1) * HD]
    seg_row = jnp.concatenate([seg_ref[...], seg_ref[...]], 1)

    def score_block(hop, top):
        column = segs[hop].T
        segc[...] = jnp.where(me >= hop, column, -1)

        def tile(t, top):
            at = pl.ds(pl.multiple_of(t * TILE, TILE), TILE)
            s = dot(kv[hop, 0, at, :], qs[...], (1, 1))
            allowed = segc[at, 0:1] == seg_row
            if hop != 1:
                k_pos = t * TILE + lax.broadcasted_iota(jnp.int32, (TILE, rows), 0)
                q_pos = lax.broadcasted_iota(jnp.int32, (TILE, rows), 1)
                inside = k_pos <= q_pos if hop == 0 else k_pos > q_pos
                allowed = allowed & jnp.concatenate([inside, inside], 1)
            s = jnp.where(allowed, s, masked_score)
            s_buf[hop, at, :] = s
            return jnp.maximum(top, jnp.max(s, 0, keepdims=True))

        return lax.fori_loop(0, tiles, tile, top)

    top = score_block(0, jnp.full((1, 2 * rows), masked_score, F32))
    if fused:
        x_copy.wait()
        wide = x_buf.shape[1]

        @pl.loop(0, wide // 128)
        def _(c):
            at = pl.ds(pl.multiple_of(c * 128, 128), 128)
            xt[at, :] = x_buf[:, at].T

    for hop in (1, 2):
        seg_copies[hop].wait()
        kv_copies[hop, 0].wait()
        top = score_block(hop, top)

    total = jnp.zeros((1, 2 * rows), F32)
    weighed = jnp.zeros((1, 2 * rows), F32)
    for hop in (0, 1, 2):
        if hop:
            kv_copies[hop, 1].wait()

        def tile(t, carry, hop=hop):
            total, weighed = carry
            at = pl.ds(pl.multiple_of(t * TILE, TILE), TILE)
            dp = dot(kv[hop, 1, at, :], dos[...], (1, 1))
            e = jnp.exp2((s_buf[hop, at, :] - top) * EXP_SCALE)
            s_buf[hop, at, :] = e
            dp_buf[hop, at, :] = dp
            return total + jnp.sum(e, 0, keepdims=True), weighed + jnp.sum(e * dp, 0, keepdims=True)

        total, weighed = lax.fori_loop(0, tiles, tile, (total, weighed))
    inverse = 1.0 / total
    delta = weighed * inverse

    g_copies = {}
    own = None
    for hop in (2, 1, 0):
        def tile(t, carry, hop=hop):
            at = pl.ds(pl.multiple_of(t * TILE, TILE), TILE)
            p = s_buf[hop, at, :] * inverse
            pb[at, :] = p.astype(BF16)
            ds[at, :] = (p * (dp_buf[hop, at, :] - delta)).astype(BF16)
            return carry

        lax.fori_loop(0, tiles, tile, 0)
        d_k = dot(ds[...], qs[...], (1, 0)) * query_scale
        d_v = dot(pb[...], dos[...], (1, 0))
        if hop:
            out_g[hop - 1, 0] = d_k.astype(BF16)
            out_g[hop - 1, 1] = d_v.astype(BF16)
            g_copies[hop] = remote(out_g.at[hop - 1], in_g.at[hop - 1], g_send.at[hop - 1], g_recv.at[hop - 1],
                                   lax.rem(me + n - hop, n))
            g_copies[hop].start()
        else:
            own = (d_k, d_v)
        dq_part = dot(kv[hop, 0].astype(F32).T.astype(BF16), ds[...], (1, 0))
        if hop == 2:
            dqt[...] = dq_part
        else:
            dqt[...] += dq_part
    for head in (0, 1):
        dq_ref[:, head * HD:(head + 1) * HD] = (
            dqt[:, head * rows:(head + 1) * rows].T * query_scale).astype(BF16)
    g_copies[2].wait()
    g_copies[1].wait()
    d_key = (own[0] + in_g[0, 0].astype(F32) + in_g[1, 0].astype(F32)).astype(BF16)
    d_value = (own[1] + in_g[0, 1].astype(F32) + in_g[1, 1].astype(F32)).astype(BF16)
    dk_ref[...] = d_key
    dv_ref[...] = d_value
    if not fused:
        return

    g_buf[:, :HD] = d_key
    g_buf[:, HD:] = d_value
    part = dwk_ref.shape[0]
    pair = me ^ 1
    side = me // 2

    def product(block):
        at = pl.ds(pl.multiple_of(block * part, 16), part)
        return dot(xt[at, :], g_buf[...], (1, 0))

    one, two, three = {}, {}, {}

    def for_pair(c):
        prod = product((side ^ c) * 2 + (pair & 1)).astype(BF16)
        one_out[c, 0] = prod[:, :HD]
        one_out[c, 1] = prod[:, HD:]
        one[c] = remote(one_out.at[c], one_in.at[c], one_send.at[c], one_recv.at[c], pair)
        one[c].start()

    def own_sum(c):
        prod = product((side ^ c) * 2 + (me & 1))
        one[c].wait()
        return prod[:, :HD] + one_in[c, 0].astype(F32), prod[:, HD:] + one_in[c, 1].astype(F32)

    over = (me ^ 2, me ^ 4)

    def send_two(half, slot, value):
        two_out[half, slot] = value.astype(BF16)
        two[half, slot] = remote(two_out.at[half, slot], two_in.at[half, slot], two_send.at[half, slot],
                                 two_recv.at[half, slot], over[half])
        two[half, slot].start()

    for_pair(3)
    for_pair(1)
    far = own_sum(3)
    send_two(0, 0, far[0])
    send_two(1, 0, far[1])
    for_pair(2)
    by_one = own_sum(1)
    send_two(0, 1, by_one[0])
    for_pair(0)
    by_two = own_sum(2)
    send_two(1, 1, by_two[1])
    mine = own_sum(0)

    def send_three(half, value):
        three_out[half] = value.astype(BF16)
        three[half] = remote(three_out.at[half], three_in.at[half], three_send.at[half], three_recv.at[half],
                             over[1 - half])
        three[half].start()

    two[0, 0].wait()
    send_three(0, by_two[0] + two_in[0, 0].astype(F32))
    two[1, 0].wait()
    send_three(1, by_one[1] + two_in[1, 0].astype(F32))
    two[0, 1].wait()
    two[1, 1].wait()
    for half, ref in ((0, dwk_ref), (1, dwv_ref)):
        ref[...] = mine[half] + two_in[half, 1].astype(F32)
    for half, ref in ((0, dwk_ref), (1, dwv_ref)):
        three[half].wait()
        ref[...] += three_in[half].astype(F32)


def body(n, tokens_in, query, key, value, d_out, seg_ids):
    rows, width = query.shape
    kv_width = key.shape[1]
    features = tokens_in.shape[1]
    part = features // n
    fused = n == 8 and part % 16 == 0
    dma = pltpu.SemaphoreType.DMA
    vmem = pltpu.VMEM
    out_shape = [
        jax.ShapeDtypeStruct((rows, width), BF16),
        jax.ShapeDtypeStruct((rows, kv_width), BF16),
        jax.ShapeDtypeStruct((rows, kv_width), BF16),
    ]
    scratch = [
        vmem((3, 2, rows, HD), BF16),
        vmem((3, 8, rows), jnp.int32),
        vmem((rows, 8), jnp.int32),
        vmem((2 * rows, HD), BF16),
        vmem((2 * rows, HD), BF16),
        vmem((3, rows, 2 * rows), F32),
        vmem((3, rows, 2 * rows), F32),
        vmem((rows, 2 * rows), BF16),
        vmem((rows, 2 * rows), BF16),
        vmem((HD, 2 * rows), F32),
        vmem((2, 2, rows, HD), BF16),
        vmem((2, 2, rows, HD), BF16),
        dma((2, 2)), dma((2, 2)), dma((2,)), dma((2,)), dma((2,)), dma((2,)),
    ]
    operands = [seg_ids.reshape(1, rows), query, key, value, d_out]
    in_specs = [pl.BlockSpec(memory_space=pltpu.VMEM)] * 5
    if fused:
        operands.append(tokens_in)
        in_specs = in_specs + [pl.BlockSpec(memory_space=pl.ANY)]
        out_shape += [jax.ShapeDtypeStruct((part, kv_width), F32)] * 2
        scratch += [
            vmem((rows, features), BF16),
            vmem((features, rows), BF16),
            vmem((rows, 2 * HD), BF16),
            vmem((4, 2, part, HD), BF16),
            vmem((4, 2, part, HD), BF16),
            vmem((2, 2, part, HD), BF16),
            vmem((2, 2, part, HD), BF16),
            vmem((2, part, HD), BF16),
            vmem((2, part, HD), BF16),
            dma((4,)), dma((4,)), dma((2, 2)), dma((2, 2)), dma((2,)), dma((2,)), dma,
        ]
    outs = pl.pallas_call(
        functools.partial(kernel, n, fused),
        out_shape=out_shape,
        in_specs=in_specs,
        out_specs=[pl.BlockSpec(memory_space=pltpu.VMEM)] * len(out_shape),
        scratch_shapes=scratch,
        compiler_params=pltpu.CompilerParams(
            collective_id=0, has_side_effects=True, vmem_limit_bytes=56 * 1024 * 1024),
    )(*operands)
    if fused:
        return tuple(outs)
    d_query, d_key, d_value = outs
    grads_both = jnp.concatenate([d_key, d_value], 1)
    summed = lax.psum_scatter(
        dot(tokens_in, grads_both, (0, 0)).astype(BF16), "ctx", scatter_dimension=0, tiled=True
    ).astype(F32)
    return (d_query, d_key, d_value, summed[:, :kv_width], summed[:, kv_width:])


def solution(mesh):
    n = mesh.shape["ctx"]
    in_specs = (P("ctx", None),) + (P("ctx", "fsdp"),) * 4 + (P("ctx"),)
    return jax.shard_map(functools.partial(body, n), mesh=mesh, in_specs=in_specs,
                         out_specs=(P("ctx", "fsdp"),) * 5, check_vma=False)
```

time: 117 us -> 54.6 us (0.47)
  waiting for transfers between devices: 51.9 us -> 0 us
  Pallas kernels: 0 us -> 45.4 us
  starting transfers between devices: 16.3 us -> 0 us
  matrix products: 15.3 us -> 0 us
  between operations: 14.5 us -> 0.64 us
  local copies, waits for them, and re-layouts: 15.4 us -> 8.26 us
  other arithmetic: 3.3 us -> 0 us
    pallas_call x0 -> x1, Pallas kernels: none -> 45.4 us  [body(): pl.pallas_call(functools.partial(kernel, n, fused), out_shape=out_shape,...]
    unnamed x2 -> x0, waiting for transfers between devices: 41.6 us -> none
    ppermute x6 -> x0, starting transfers between devices: 16.3 us -> none  [shifted(): return lax.ppermute(array, axis, pairs)]
    dot_general x19 -> x0, matrix products: 15.3 us -> none  [the longest x3 3.19 us: block_grads(): jnp.einsum('ihgd,jhd->hgij', grad_heads, values, preferred_element_type=j...]
    ppermute x6 -> x0, waiting for transfers between devices: 10.3 us -> none  [shifted(): return lax.ppermute(array, axis, pairs)]
    unnamed x28 -> x5, local copies, waits for them, and re-layouts: 11 us -> 8.26 us
    another operation x2 -> x0, local copies, waits for them, and re-layouts: 2.18 us -> none
    and x1 -> x0, other arithmetic: 1.54 us -> none  [body(): allowed & (k_pos[None, :] >= 0) & (seg_ids[:, None] == block_seg[None, :])]
  transfers between devices with their start and end apart: 7 -> 0, of which waited for: 2 -> 0; matrix products, arithmetic and copies ran while one was open for 13% -> 0% of each run, Pallas kernels for 0% -> 0%
where the time goes in v1:
time: 54.6 us; the launch traced here: 54.3 us
  Pallas kernels  45.4 us (83%)
  local copies, waits for them, and re-layouts  8.26 us (15%)
  between operations  0.64 us (1%)
    pallas_call x1, Pallas kernels, body(): pl.pallas_call(functools.partial(kernel, n, fused), out_shape=out_shape,...  45.4 us
    unnamed x5, local copies, waits for them, and re-layouts  8.26 us

profile of v1, /device:TPU:0, one launch (start us, length us, event | category | flops | bytes accessed | tf_op | source)
XLA Modules:
  0.0 54.3 jit_solution(8208846125167983633)
XLA Ops:
  0.6 45.4 %shard_map.101 = (bf16[512,256]{1,0:T(8,128)(2,1)}, bf16[512,128]{1,0:T(8,128)(2,1)}, bf16[512,128]{1,0:T(8,128)(2,1)}, f32[672,128]{1,0:T(8,128)}, f32[672,128]{1,0:T(8,128)}) custom-call(s32[1,512]{1,0:T(1,128)} %bitcast.1, bf16[512,256]{1,0:T(8,128)(2,1)} %refs_1_.1, bf16[512,128]{1,0:T(8,128)(2,1)} %refs_2_.1, bf16[512,128]{1,0:T(8,128)(2,1)} %refs_3_.1, ...), custom_call_target="tpu_custom_call" | custom-call | tf_op jit(solution)/shard_map/pallas_call | solution.py:277
  46.0 1.7 %copy.16 = bf16[512,256]{1,0:T(8,128)(2,1)} copy(bf16[512,256]{1,0:T(8,128)(2,1)} %get-tuple-element.10) | data formatting | bytes 524288
  47.7 1.6 %copy.17 = bf16[512,128]{1,0:T(8,128)(2,1)} copy(bf16[512,128]{1,0:T(8,128)(2,1)} %get-tuple-element.11) | data formatting | bytes 262144
  49.2 1.6 %copy.18 = bf16[512,128]{1,0:T(8,128)(2,1)} copy(bf16[512,128]{1,0:T(8,128)(2,1)} %get-tuple-element.12) | data formatting | bytes 262144
  50.8 1.7 %copy.19 = f32[672,128]{1,0:T(8,128)} copy(f32[672,128]{1,0:T(8,128)} %get-tuple-element.13) | data formatting | bytes 688128
  52.5 1.7 %copy.20 = f32[672,128]{1,0:T(8,128)} copy(f32[672,128]{1,0:T(8,128)} %get-tuple-element.14) | data formatting | bytes 688128

commit v2 on v1

--- a/solution.py
+++ b/solution.py
@@ -73,12 +73,16 @@
         dos[pl.ds(head * rows, rows), :] = do_ref[:, head * HD:(head + 1) * HD]
     seg_row = jnp.concatenate([seg_ref[...], seg_ref[...]], 1)
 
+    def by_tiles(step, carry):
+        def tile(t, carry):
+            return step(t, pl.ds(pl.multiple_of(t * TILE, TILE), TILE), carry)
+
+        return lax.fori_loop(0, tiles, tile, carry)
+
     def score_block(hop, top):
-        column = segs[hop].T
-        segc[...] = jnp.where(me >= hop, column, -1)
-
-        def tile(t, top):
-            at = pl.ds(pl.multiple_of(t * TILE, TILE), TILE)
+        segc[...] = jnp.where(me >= hop, segs[hop].T, -1)
+
+        def step(t, at, top):
             s = dot(kv[hop, 0, at, :], qs[...], (1, 1))
             allowed = segc[at, 0:1] == seg_row
             if hop != 1:
@@ -90,64 +94,78 @@
             s_buf[hop, at, :] = s
             return jnp.maximum(top, jnp.max(s, 0, keepdims=True))
 
-        return lax.fori_loop(0, tiles, tile, top)
-
-    top = score_block(0, jnp.full((1, 2 * rows), masked_score, F32))
-    if fused:
-        x_copy.wait()
-        wide = x_buf.shape[1]
-
-        @pl.loop(0, wide // 128)
+        return by_tiles(step, top)
+
+    def turn_tokens(first, last):
+        @pl.loop(first, last)
         def _(c):
             at = pl.ds(pl.multiple_of(c * 128, 128), 128)
             xt[at, :] = x_buf[:, at].T
 
+    top = score_block(0, jnp.full((1, 2 * rows), masked_score, F32))
+    if fused:
+        blocks = x_buf.shape[1] // 128
+        early = blocks // 2
+        x_copy.wait()
+        turn_tokens(0, early)
     for hop in (1, 2):
         seg_copies[hop].wait()
         kv_copies[hop, 0].wait()
         top = score_block(hop, top)
 
     total = jnp.zeros((1, 2 * rows), F32)
-    weighed = jnp.zeros((1, 2 * rows), F32)
+    for hop in (0, 1, 2):
+        def step(t, at, total, hop=hop):
+            e = jnp.exp2((s_buf[hop, at, :] - top) * EXP_SCALE)
+            s_buf[hop, at, :] = e
+            return total + jnp.sum(e, 0, keepdims=True)
+
+        total = by_tiles(step, total)
+    inverse = 1.0 / total
+
+    g_copies = {}
+    own = {}
+
+    def give(hop, which, value):
+        if hop == 0:
+            own[which] = value
+            return
+        out_g[hop - 1, which] = value.astype(BF16)
+        g_copies[hop, which] = remote(out_g.at[hop - 1, which], in_g.at[hop - 1, which], g_send.at[hop - 1, which],
+                                      g_recv.at[hop - 1, which], lax.rem(me + n - hop, n))
+        g_copies[hop, which].start()
+
+    for hop in (2, 1, 0):
+        def step(t, at, carry, hop=hop):
+            p = s_buf[hop, at, :] * inverse
+            s_buf[hop, at, :] = p
+            pb[at, :] = p.astype(BF16)
+            return carry
+
+        by_tiles(step, 0)
+        give(hop, 1, dot(pb[...], dos[...], (1, 0)))
+
+    delta = jnp.zeros((1, 2 * rows), F32)
     for hop in (0, 1, 2):
         if hop:
             kv_copies[hop, 1].wait()
 
-        def tile(t, carry, hop=hop):
-            total, weighed = carry
-            at = pl.ds(pl.multiple_of(t * TILE, TILE), TILE)
+        def step(t, at, delta, hop=hop):
             dp = dot(kv[hop, 1, at, :], dos[...], (1, 1))
-            e = jnp.exp2((s_buf[hop, at, :] - top) * EXP_SCALE)
-            s_buf[hop, at, :] = e
             dp_buf[hop, at, :] = dp
-            return total + jnp.sum(e, 0, keepdims=True), weighed + jnp.sum(e * dp, 0, keepdims=True)
-
-        total, weighed = lax.fori_loop(0, tiles, tile, (total, weighed))
-    inverse = 1.0 / total
-    delta = weighed * inverse
-
-    g_copies = {}
-    own = None
+            return delta + jnp.sum(s_buf[hop, at, :] * dp, 0, keepdims=True)
+
+        delta = by_tiles(step, delta)
+
     for hop in (2, 1, 0):
-        def tile(t, carry, hop=hop):
-            at = pl.ds(pl.multiple_of(t * TILE, TILE), TILE)
-            p = s_buf[hop, at, :] * inverse
-            pb[at, :] = p.astype(BF16)
-            ds[at, :] = (p * (dp_buf[hop, at, :] - delta)).astype(BF16)
+        def step(t, at, carry, hop=hop):
+            ds[hop, at, :] = (s_buf[hop, at, :] * (dp_buf[hop, at, :] - delta)).astype(BF16)
             return carry
 
-        lax.fori_loop(0, tiles, tile, 0)
-        d_k = dot(ds[...], qs[...], (1, 0)) * query_scale
-        d_v = dot(pb[...], dos[...], (1, 0))
-        if hop:
-            out_g[hop - 1, 0] = d_k.astype(BF16)
-            out_g[hop - 1, 1] = d_v.astype(BF16)
-            g_copies[hop] = remote(out_g.at[hop - 1], in_g.at[hop - 1], g_send.at[hop - 1], g_recv.at[hop - 1],
-                                   lax.rem(me + n - hop, n))
-            g_copies[hop].start()
-        else:
-            own = (d_k, d_v)
-        dq_part = dot(kv[hop, 0].astype(F32).T.astype(BF16), ds[...], (1, 0))
+        by_tiles(step, 0)
+        give(hop, 0, dot(ds[hop], qs[...], (1, 0)) * query_scale)
+    for hop in (2, 1, 0):
+        dq_part = dot(kv[hop, 0].astype(F32).T.astype(BF16), ds[hop], (1, 0))
         if hop == 2:
             dqt[...] = dq_part
         else:
@@ -155,8 +173,11 @@
     for head in (0, 1):
         dq_ref[:, head * HD:(head + 1) * HD] = (
             dqt[:, head * rows:(head + 1) * rows].T * query_scale).astype(BF16)
-    g_copies[2].wait()
-    g_copies[1].wait()
+    if fused:
+        turn_tokens(early, blocks)
+    for which in (1, 0):
+        for hop in (2, 1):
+            g_copies[hop, which].wait()
     d_key = (own[0] + in_g[0, 0].astype(F32) + in_g[1, 0].astype(F32)).astype(BF16)
     d_value = (own[1] + in_g[0, 1].astype(F32) + in_g[1, 1].astype(F32)).astype(BF16)
     dk_ref[...] = d_key
@@ -226,6 +247,12 @@
     for half, ref in ((0, dwk_ref), (1, dwv_ref)):
         three[half].wait()
         ref[...] += three_in[half].astype(F32)
+
+
+def hand_on(*refs):
+    count = len(refs) // 2
+    for i in range(count):
+        refs[count + i][...] = refs[i][...]
 
 
 def body(n, tokens_in, query, key, value, d_out, seg_ids):
@@ -250,11 +277,11 @@
         vmem((3, rows, 2 * rows), F32),
         vmem((3, rows, 2 * rows), F32),
         vmem((rows, 2 * rows), BF16),
-        vmem((rows, 2 * rows), BF16),
+        vmem((3, rows, 2 * rows), BF16),
         vmem((HD, 2 * rows), F32),
         vmem((2, 2, rows, HD), BF16),
         vmem((2, 2, rows, HD), BF16),
-        dma((2, 2)), dma((2, 2)), dma((2,)), dma((2,)), dma((2,)), dma((2,)),
+        dma((2, 2)), dma((2, 2)), dma((2,)), dma((2,)), dma((2, 2)), dma((2, 2)),
     ]
     operands = [seg_ids.reshape(1, rows), query, key, value, d_out]
     in_specs = [pl.BlockSpec(memory_space=pltpu.VMEM)] * 5
@@ -284,7 +311,10 @@
             collective_id=0, has_side_effects=True, vmem_limit_bytes=56 * 1024 * 1024),
     )(*operands)
     if fused:
-        return tuple(outs)
+        whole = pl.BlockSpec(memory_space=pltpu.VMEM)
+        return tuple(pl.pallas_call(
+            hand_on, out_shape=out_shape, in_specs=[whole] * 5, out_specs=[whole] * 5,
+        )(*outs))
     d_query, d_key, d_value = outs
     grads_both = jnp.concatenate([d_key, d_value], 1)
     summed = lax.psum_scatter(

time: 54.6 us -> 45.9 us (0.84)
  local copies, waits for them, and re-layouts: 8.26 us -> 0 us
    unnamed x5 -> x0, local copies, waits for them, and re-layouts: 8.26 us -> none
    pallas_call x1, Pallas kernels: 45.4 us -> 42.8 us  [body(): pl.pallas_call(functools.partial(kernel, n, fused), out_shape=out_shape,...]
    pallas_call x0 -> x1, Pallas kernels: none -> 2.3 us  [body(): pl.pallas_call(hand_on, out_shape=out_shape, in_specs=[whole] * 5, out_sp...]
where the time goes in v2:
time: 45.9 us; the launch traced here: 45.7 us
  Pallas kernels  45.1 us (98%)
  between operations  0.64 us (1%)
    pallas_call x1, Pallas kernels, body(): pl.pallas_call(functools.partial(kernel, n, fused), out_shape=out_shape,...  42.8 us
    pallas_call x1, Pallas kernels, body(): pl.pallas_call(hand_on, out_shape=out_shape, in_specs=[whole] * 5, out_sp...  2.3 us

profile of v2, /device:TPU:0, one launch (start us, length us, event | category | flops | bytes accessed | tf_op | source)
XLA Modules:
  0.0 45.7 jit_solution(6789057973402713168)
XLA Ops:
  0.6 42.8 %shard_map.101 = (bf16[512,256]{1,0:T(8,128)(2,1)}, bf16[512,128]{1,0:T(8,128)(2,1)}, bf16[512,128]{1,0:T(8,128)(2,1)}, f32[672,128]{1,0:T(8,128)}, f32[672,128]{1,0:T(8,128)}) custom-call(s32[1,512]{1,0:T(1,128)} %bitcast.1, bf16[512,256]{1,0:T(8,128)(2,1)} %refs_1_.1, bf16[512,128]{1,0:T(8,128)(2,1)} %refs_2_.1, bf16[512,128]{1,0:T(8,128)(2,1)} %refs_3_.1, ...), custom_call_target="tpu_custom_call" | custom-call | tf_op jit(solution)/shard_map/pallas_call | solution.py:304
  43.4 2.3 %shard_map.102 = (bf16[512,256]{1,0:T(8,128)(2,1)}, bf16[512,128]{1,0:T(8,128)(2,1)}, bf16[512,128]{1,0:T(8,128)(2,1)}, f32[672,128]{1,0:T(8,128)}, f32[672,128]{1,0:T(8,128)}) custom-call(bf16[512,256]{1,0:T(8,128)(2,1)} %get-tuple-element.10.refs_0_, bf16[512,128]{1,0:T(8,128)(2,1)} %get-tuple-element.11.refs_1_, ...), custom_call_target="tpu_custom_call" | custom-call | tf_op jit(solution)/shard_map/pallas_call | solution.py:315

commit v3 on v2

--- a/solution.py
+++ b/solution.py
@@ -77,7 +77,7 @@
         def tile(t, carry):
             return step(t, pl.ds(pl.multiple_of(t * TILE, TILE), TILE), carry)
 
-        return lax.fori_loop(0, tiles, tile, carry)
+        return lax.fori_loop(0, tiles, tile, carry, unroll=2)
 
     def score_block(hop, top):
         segc[...] = jnp.where(me >= hop, segs[hop].T, -1)
@@ -137,9 +137,7 @@
 
     for hop in (2, 1, 0):
         def step(t, at, carry, hop=hop):
-            p = s_buf[hop, at, :] * inverse
-            s_buf[hop, at, :] = p
-            pb[at, :] = p.astype(BF16)
+            pb[at, :] = (s_buf[hop, at, :] * inverse).astype(BF16)
             return carry
 
         by_tiles(step, 0)
@@ -156,10 +154,11 @@
             return delta + jnp.sum(s_buf[hop, at, :] * dp, 0, keepdims=True)
 
         delta = by_tiles(step, delta)
+    delta = delta * inverse
 
     for hop in (2, 1, 0):
         def step(t, at, carry, hop=hop):
-            ds[hop, at, :] = (s_buf[hop, at, :] * (dp_buf[hop, at, :] - delta)).astype(BF16)
+            ds[hop, at, :] = (s_buf[hop, at, :] * inverse * (dp_buf[hop, at, :] - delta)).astype(BF16)
             return carry
 
         by_tiles(step, 0)

time: 45.9 us -> 44.4 us (0.967)
  Pallas kernels: 45.1 us -> 43.6 us
    pallas_call x1, Pallas kernels: 42.8 us -> 41.3 us  [body(): pl.pallas_call(functools.partial(kernel, n, fused), out_shape=out_shape,...]
where the time goes in v3:
time: 44.4 us; the launch traced here: 44.3 us
  Pallas kernels  43.6 us (98%)
  between operations  0.64 us (1%)
    pallas_call x1, Pallas kernels, body(): pl.pallas_call(functools.partial(kernel, n, fused), out_shape=out_shape,...  41.3 us
    pallas_call x1, Pallas kernels, body(): pl.pallas_call(hand_on, out_shape=out_shape, in_specs=[whole] * 5, out_sp...  2.3 us

profile of v3, /device:TPU:0, one launch (start us, length us, event | category | flops | bytes accessed | tf_op | source)
XLA Modules:
  0.0 44.3 jit_solution(11460069395717662532)
XLA Ops:
  0.6 41.3 %shard_map.101 = (bf16[512,256]{1,0:T(8,128)(2,1)}, bf16[512,128]{1,0:T(8,128)(2,1)}, bf16[512,128]{1,0:T(8,128)(2,1)}, f32[672,128]{1,0:T(8,128)}, f32[672,128]{1,0:T(8,128)}) custom-call(s32[1,512]{1,0:T(1,128)} %bitcast.1, bf16[512,256]{1,0:T(8,128)(2,1)} %refs_1_.1, bf16[512,128]{1,0:T(8,128)(2,1)} %refs_2_.1, bf16[512,128]{1,0:T(8,128)(2,1)} %refs_3_.1, ...), custom_call_target="tpu_custom_call" | custom-call | tf_op jit(solution)/shard_map/pallas_call | solution.py:303
  42.0 2.3 %shard_map.102 = (bf16[512,256]{1,0:T(8,128)(2,1)}, bf16[512,128]{1,0:T(8,128)(2,1)}, bf16[512,128]{1,0:T(8,128)(2,1)}, f32[672,128]{1,0:T(8,128)}, f32[672,128]{1,0:T(8,128)}) custom-call(bf16[512,256]{1,0:T(8,128)(2,1)} %get-tuple-element.10.refs_0_, bf16[512,128]{1,0:T(8,128)(2,1)} %get-tuple-element.11.refs_1_, ...), custom_call_target="tpu_custom_call" | custom-call | tf_op jit(solution)/shard_map/pallas_call | solution.py:314
